TPU v7x, 128 devices: a whole 4x4x4 slice. The times are simulated.
128 devices in a mesh: group: 8 (over z, core), tensor: 16 (over y, x).
Axes of the slice: x: 4, y: 4, z: 4, core: 2. Of those that a mesh axis runs over, the one named last changes fastest.
Arguments:
- panel: bfloat16 [16384, 7168], P('group', 'tensor'), may hold values from -1.5 to 1.5, as said below
- hidden: bfloat16 [8192, 7168], P('group'), may hold values from -9 to 9
- targets: int32 [8192], P('group'), may hold values from 0 to 16383
- counts: int32 [8], P('group'), may hold values from 512 to 1024, as said below
Outputs:
- logprob: float32 [8192], P('group')
- rollout_panel: bfloat16 [16384, 7168], P('tensor')
- rollout_scale: bfloat16 [128, 56], P('tensor')
Inputs may be any that keep to these rules, and one draw needn't show every extreme that they name: `counts`: live rows of one replica; at least one replica is full in every draw. `panel`: entries lie within 12 / sqrt(7168) in magnitude.
All inputs are finite; a program needn't handle non-finite values.
Results may differ from a plain program's by a relative error of at most 0.0052.
Values may be sent and summed in bfloat16 or wider, within the bound.
A program may use at most 192 MiB of HBM per device.

v0:
```python
import jax
import jax.numpy as jnp
from jax import lax
from jax.sharding import PartitionSpec as P

V_PANEL = 16384
QBLOCK = 128


def quantize(rows):
    count, width = rows.shape
    blocks = rows.astype(jnp.float32).reshape(count // QBLOCK, QBLOCK, width // QBLOCK, QBLOCK)
    largest = jnp.max(jnp.abs(blocks), axis=(1, 3))
    scale = ((largest + 1e-06) / 448.0).astype(jnp.bfloat16)
    spread = scale.astype(jnp.float32)[:, None, :, None]
    quant = (blocks / spread).astype(jnp.bfloat16)
    return (quant.reshape(count, width), scale)


def dequantize(quant, scale):
    count, width = quant.shape
    held = lax.optimization_barrier(quant)
    blocks = held.astype(jnp.float32).reshape(count // QBLOCK, QBLOCK, width // QBLOCK, QBLOCK)
    spread = scale.astype(jnp.float32)[:, None, :, None]
    return (blocks * spread).astype(jnp.bfloat16).reshape(count, width)


def local(panel, hidden, targets, counts):
    groups = lax.axis_size("group")
    tens = lax.axis_size("tensor")
    sub = V_PANEL // (groups * tens)
    rows = lax.all_gather(panel, "group", axis=0, tiled=True)
    width = rows.shape[1]
    rows = rows.reshape(groups, tens, sub, width).transpose(1, 0, 2, 3).reshape(V_PANEL, width)
    sliver = lax.all_to_all(rows, "tensor", split_axis=0, concat_axis=1, tiled=True)
    quant, scale = quantize(sliver)
    weights = dequantize(quant, scale)
    logits = lax.dot_general(
        hidden, weights, (((1,), (1,)), ((), ())), preferred_element_type=jnp.float32
    )
    column = jnp.arange(weights.shape[0], dtype=jnp.int32)
    vocab = column // sub * (tens * sub) + lax.axis_index("tensor") * sub + column % sub
    picked = jnp.sum(jnp.where(vocab[None, :] == targets[:, None], logits, 0.0), axis=1)
    local_top = jnp.max(logits, axis=1)
    top = lax.pmax(local_top, "tensor")
    local_sum = jnp.sum(jnp.exp(logits - top[:, None]), axis=1)
    total, target_logit = lax.psum((local_sum, picked), "tensor")
    lse = top + jnp.log(total)
    live = jnp.arange(hidden.shape[0], dtype=jnp.int32) < counts[0]
    logprob = jnp.where(live, target_logit - lse, jnp.float32(0.0))
    return (logprob, quant, scale)


def solution(mesh):
    in_specs = (P("group", "tensor"), P("group", None), P("group"), P("group"))
    out_specs = (P("group"), P("tensor", None), P("tensor", None))
    return jax.shard_map(local, mesh=mesh, in_specs=in_specs, out_specs=out_specs, check_vma=False)
```

profile of v0, /device:TPU:0, one launch (start us, length us, event | category | flops | bytes accessed | tf_op | source)
XLA Modules:
  0.0 560.8 jit_solution(7705525044878425014)
XLA Ops:
  7.2 0.0 all-gather.2.cloned.1.call-start
  7.2 0.7 all-gather.2.cloned.1.call-update
  7.9 80.6 %all-gather.2.cloned.1.call-done = bf16[16384,448]{0,1:T(8,128)(2,1)} async-done(((bf16[2048,448]{0,1:T(8,128)(2,1)}), bf16[16384,448]{0,1:T(8,128)(2,1)}) %all-gather.2.cloned.1.call-update) | async-done | bytes 14680080 | tf_op jit(solution)/shard_map/all_gather | solution.py:32
  88.5 8.8 %copy.14 = bf16[56,8,128,128]{3,2,1,0:T(8,128)(2,1)S(1)} copy(bf16[56,8,128,128]{3,1,2,0:T(8,128)(2,1)} %bitcast.55) | data formatting | bytes 29360128
  97.3 7.2 %copy.23 = bf16[8,16,128,448]{2,0,3,1:T(8,128)(2,1)} copy(bf16[8,16,128,448]{2,1,0,3:T(8,128)(2,1)S(1)} %bitcast.53) | data formatting | bytes 29360128 | tf_op jit(solution)/shard_map/reshape | solution.py:34
  104.5 22.3 %all_to_all.10 = bf16[16,1024,448]{1,2,0:T(8,128)(2,1)} reshape(bf16[16,8,128,448]{2,1,3,0:T(8,128)(2,1)} %bitcast.54) | data formatting | bytes 29360128 | tf_op jit(solution)/shard_map/all_to_all | solution.py:35
  126.9 6.9 %all-to-all-start = ((bf16[16,1024,448]{1,2,0:T(8,128)(2,1)}), bf16[16,1024,448]{1,2,0:T(8,128)(2,1)}, u32[]{:S(2)}, u32[]{:S(2)}) async-start(bf16[16,1024,448]{1,2,0:T(8,128)(2,1)} %all_to_all.10), calls=%async_computation | async-start | bytes 29360128 | tf_op jit(solution)/shard_map/all_to_all | solution.py:35
  134.4 219.6 %all-to-all-done = bf16[16,1024,448]{1,2,0:T(8,128)(2,1)} async-done(((bf16[16,1024,448]{1,2,0:T(8,128)(2,1)}), bf16[16,1024,448]{1,2,0:T(8,128)(2,1)}, u32[]{:S(2)}, u32[]{:S(2)}) %all-to-all-start) | async-done | bytes 14680096 | tf_op jit(solution)/shard_map/all_to_all | solution.py:35
  354.0 9.0 %convert_abs_fusion = f32[16,1024,448]{1,2,0:T(8,128)S(1)} fusion(bf16[16,1024,448]{1,2,0:T(8,128)(2,1)} %all-to-all-done), kind=kLoop, calls=%fused_computation.6 | loop fusion | flops 14680064 | bytes 44040192 | tf_op jit(solution)/shard_map/abs | solution.py:13
  363.0 13.5 %copy.15 = f32[896,8,8,128]{3,2,1,0:T(8,128)} copy(f32[896,8,8,128]{3,1,2,0:T(8,128)S(1)} %bitcast.52) | data formatting | bytes 58720256
  376.4 10.9 %reduce_max.18 = f32[8,56]{0,1:T(8,128)S(1)} reduce(f32[8,128,56,128]{1,0,3,2:T(8,128)} %bitcast.51, f32[]{:T(128)} %constant.42.clone.1), dimensions={1,3}, to_apply=%region_0.0 | reduce | flops 7339584 | bytes 29361924 | tf_op jit(solution)/shard_map/reduce_max | solution.py:13
  387.3 11.6 %div.29 = f32[8,128,56,128]{1,0,3,2:T(8,128)} broadcast(bf16[8,56]{0,1:T(8,128)(2,1)S(1)} %multiply_convert_fusion), dimensions={0,2} | broadcast | bytes 29361024 | tf_op jit(solution)/shard_map/div | solution.py:16
  398.9 23.4 %fusion = bf16[1024,7168]{0,1:T(8,128)(2,1)} fusion(f32[896,8,8,128]{3,2,1,0:T(8,128)} %bitcast.49, bf16[16,1024,448]{1,2,0:T(8,128)(2,1)} %all-to-all-done), kind=kLoop, calls=%fused_computation.2 | loop fusion | flops 22020096 | bytes 58720256 | tf_op jit(solution)/shard_map/convert_element_type | solution.py:16
  422.3 19.9 %copy.12 = bf16[1024,7168]{1,0:T(8,128)(2,1)} copy(bf16[1024,7168]{0,1:T(8,128)(2,1)} %fusion) | data formatting | bytes 29360128
  442.2 0.7 copy.13
  442.9 0.0 copy-start
  442.9 34.1 %fusion.17 = (f32[1024]{0:T(1024)S(1)}, f32[1024,1024]{1,0:T(8,128)}) fusion(bf16[1024,7168]{1,0:T(8,128)(2,1)} %param.5, bf16[1024,7168]{0,1:T(8,128)(2,1)} %fusion, f32[896,8,8,128]{3,2,1,0:T(8,128)} %bitcast.50), kind=kOutput, calls=%fused_computation.29 | convolution fusion | flops 15055453184 | bytes 62918656 | tf_op jit(solution)/shard_map/dot_general | solution.py:38
  477.0 35.4 %pmax.7 = f32[1024]{0:T(1024)S(1)} all-reduce(f32[1024]{0:T(1024)S(1)} %get-tuple-element.13), channel_id=1, replica_groups=mesh['group'=8,'tensor'=16] {'tensor'}, use_global_device_ids=true, to_apply=%region_4.5 | all-reduce | flops 1024 | bytes 8192 | tf_op jit(solution)/shard_map/pmax | solution.py:45
  512.5 0.0 copy-done
  512.5 2.8 fusion.6
  515.3 38.0 %all-reduce = (f32[1024]{0:T(1024)S(1)}, f32[1024]{0:T(1024)S(1)}) all-reduce(f32[1024]{0:T(1024)S(1)} %get-tuple-element.10, f32[1024]{0:T(1024)S(1)} %get-tuple-element.9), channel_id=1, replica_groups=mesh['group'=8,'tensor'=16] {'tensor'}, use_global_device_ids=true, to_apply=%region_2.3 | all-reduce | flops 2048 | bytes 16384 | tf_op jit(solution)/shard_map/psum | solution.py:47
  553.3 0.6 subtract_select_fusion
  (2 shorter events, 0.0 us)
Async XLA Ops:
  7.2 81.4 %all-gather.2.cloned.1.call-start = ((), (), s32[]{:S(2)}) async-start(), calls=%async_computation.1 | async-start | bytes 16515072 | tf_op jit(solution)/shard_map/all_gather | solution.py:32
  126.9 227.2 %all-to-all-start = ((bf16[16,1024,448]{1,2,0:T(8,128)(2,1)}), bf16[16,1024,448]{1,2,0:T(8,128)(2,1)}, u32[]{:S(2)}, u32[]{:S(2)}) async-start(bf16[16,1024,448]{1,2,0:T(8,128)(2,1)} %all_to_all.10), calls=%async_computation | async-start | bytes 29360128 | tf_op jit(solution)/shard_map/all_to_all | solution.py:35
  442.9 69.6 %copy-start = (s32[1024]{0:T(1024)S(1)}, s32[1024]{0:T(1024)}, u32[]{:S(2)}) copy-start(s32[1024]{0:T(1024)} %param.6) | copy-start | bytes 12292
Sparse Core Ops, SparseCore 0:
  9.7 78.7 all-gather.1
where the time goes:
time: 562 us; the launch traced here: 561 us
  waiting for transfers between devices  301 us (54%)
  local copies, waits for them, and re-layouts  84 us (15%)
  blocking collectives  73.4 us (13%)
  other arithmetic  46.7 us (8%)
  matrix products  34.1 us (6%)
  between operations  14.7 us (3%)
  starting transfers between devices  6.89 us (1%)
    all_to_all x1, waiting for transfers between devices, local(): lax.all_to_all(rows, 'tensor', split_axis=0, concat_axis=1, tiled=True)  220 us
    all_gather x1, waiting for transfers between devices, local(): rows = lax.all_gather(panel, 'group', axis=0, tiled=True)  80.6 us
    unnamed x6, local copies, waits for them, and re-layouts  42.8 us
    psum x1, blocking collectives, local(): total, target_logit = lax.psum((local_sum, picked), 'tensor')  38 us
    pmax x1, blocking collectives, local(): top = lax.pmax(local_top, 'tensor')  35.4 us
    dot_general x1, matrix products, local(): lax.dot_general(hidden, weights, (((1,), (1,)), ((), ())), preferred_elem...  34.1 us
    convert_element_type x1, other arithmetic, quantize(): quant = (blocks / spread).astype(jnp.bfloat16)  23.4 us
    all_to_all x1, local copies, waits for them, and re-layouts, local(): lax.all_to_all(rows, 'tensor', split_axis=0, concat_axis=1, tiled=True)  22.3 us
  transfers between devices with their start and end apart: 2, of which 2 were waited for; matrix products, arithmetic and copies ran while one was open for 0% of the time, Pallas kernels for 0%

commit v1 on v0

v1 whole, which is shorter than its diff:
```python
import functools

import jax
import jax.numpy as jnp
from jax import lax
from jax.experimental import pallas as pl
from jax.experimental.pallas import tpu as pltpu
from jax.sharding import PartitionSpec as P

MESH = pl.DeviceIdType.MESH
QB = 128
NZ = 4
NG = 8
NT = 16
NP = 8
ROWS = 1024
D = 7168
SRC = D // NT
CW = 2 * SRC
BLOCKS = CW // QB
HALF = QB // 2


def kernel(
    panel, hidden, targets, counts,
    logprob, quant, scale,
    arrived, states, scales, logits, stats,
    a2a_send, a2a_recv, hid_sem,
    own_send, fwd_send, core_send, sc_send, st_send,
    prev_recv, next_recv, top_recv, bot_recv, core_recv, sc_recv, st_recv,
):
    g = lax.axis_index("group")
    t = lax.axis_index("tensor")
    z, c = g // 2, g % 2
    gp = lax.rem(z + 3, NZ) * 2 + c
    gn = lax.rem(z + 1, NZ) * 2 + c
    gf = lax.rem(z + 2, NZ) * 2 + c
    go = z * 2 + 1 - c
    p0 = t // 2

    def pair(k):
        return lax.rem(p0 + k, NP)

    def cols(p):
        return pl.ds(pl.multiple_of(p * CW, CW), CW)

    def rows(b, first=0, size=QB):
        return pl.ds(pl.multiple_of(b * QB + first, HALF), size)

    def tens(u):
        return pl.ds(pl.multiple_of(u * QB, QB), QB)

    def block_of(u):
        return pl.ds(pl.multiple_of(u * SRC, SRC), SRC)

    def wait(ref, sem):
        pltpu.make_async_copy(ref, ref, sem).wait()

    def remote(src, dst, send, recv, to):
        pltpu.make_async_remote_copy(
            src_ref=src, dst_ref=dst, send_sem=send, recv_sem=recv, device_id=to, device_id_type=MESH
        ).start()

    pltpu.make_async_copy(panel.at[:, tens(t)], arrived.at[block_of(t)], a2a_recv.at[t]).start()
    barrier = pltpu.get_barrier_semaphore()

    @pl.loop(1, NT)
    def _(s):
        pl.semaphore_signal(barrier, inc=1, device_id=(g, lax.rem(t + s, NT)), device_id_type=MESH)

    @pl.loop(1, NG)
    def _(s):
        pl.semaphore_signal(barrier, inc=1, device_id=(lax.rem(g + s, NG), t), device_id_type=MESH)

    pl.semaphore_wait(barrier, NT - 1 + NG - 1)

    def send_block(u):
        remote(panel.at[:, tens(u)], arrived.at[block_of(t)], a2a_send.at[u], a2a_recv.at[t], (g, u))

    send_block(2 * p0 + 1 - lax.rem(t, 2))

    @pl.loop(1, NP)
    def _(j):
        q = lax.rem(p0 + NP - j, NP)
        send_block(2 * q)
        send_block(2 * q + 1)

    pltpu.make_async_copy(hidden, states, hid_sem).start()
    logits[...] = jnp.zeros_like(logits)

    def step_own(k):
        p = pair(k)
        wait(arrived.at[block_of(2 * p)], a2a_recv.at[2 * p])
        wait(arrived.at[block_of(2 * p + 1)], a2a_recv.at[2 * p + 1])
        lane = lax.broadcasted_iota(jnp.int32, (8, QB), 1)
        tile = jnp.zeros((8, QB), jnp.float32)
        for i in range(BLOCKS):
            block = arrived[pl.ds(pl.multiple_of(p * CW + i * QB, QB), QB)].astype(jnp.float32)
            largest = jnp.max(jnp.abs(block), axis=(0, 1), keepdims=True)
            s = ((largest + 1e-06) / 448.0).astype(jnp.bfloat16).astype(jnp.float32)
            q = (block / s).astype(jnp.bfloat16).T
            quant[rows(g), pl.ds(pl.multiple_of(p * CW + i * QB, QB), QB)] = q
            tile = jnp.where(lane == i, jnp.broadcast_to(s, (8, QB)), tile)
        scales[p, g] = tile
        block = quant.at[rows(g), cols(p)]
        remote(block, block, own_send.at[0, k], prev_recv.at[k], (gn, t))
        remote(block, block, own_send.at[1, k], next_recv.at[k], (gp, t))
        remote(block, block, core_send.at[0, k], core_recv.at[0, k], (go, t))

        @pl.loop(1, NG)
        def _(s):
            remote(scales.at[p, g], scales.at[p, g], sc_send.at[k], sc_recv.at[k], (lax.rem(g + s, NG), t))

    def step_near(k):
        p = pair(k)
        block = quant.at[rows(gp), cols(p)]
        wait(block, prev_recv.at[k])
        top = quant.at[rows(gp, 0, HALF), cols(p)]
        remote(top, top, fwd_send.at[0, k], top_recv.at[k], (gn, t))
        remote(block, block, core_send.at[1, k], core_recv.at[1, k], (go, t))
        block = quant.at[rows(gn), cols(p)]
        wait(block, next_recv.at[k])
        bot = quant.at[rows(gn, HALF, HALF), cols(p)]
        remote(bot, bot, fwd_send.at[1, k], bot_recv.at[k], (gp, t))
        remote(block, block, core_send.at[2, k], core_recv.at[2, k], (go, t))

    def step_far(k):
        p = pair(k)
        wait(quant.at[rows(gf, 0, HALF), cols(p)], top_recv.at[k])
        wait(quant.at[rows(gf, HALF, HALF), cols(p)], bot_recv.at[k])
        block = quant.at[rows(gf), cols(p)]
        remote(block, block, core_send.at[3, k], core_recv.at[3, k], (go, t))

    def step_dot(k):
        p = pair(k)
        wait(scales.at[0, pl.ds(0, NG - 1)], sc_recv.at[k])
        chunk = quant.at[rows(0), cols(p)]
        for n in range(4):
            wait(chunk, core_recv.at[n, k])

        @pl.loop(0, NZ)
        def _(j):
            b = lax.rem(z + j, NZ)
            parts = []
            for h in range(2):
                s = scales[p, 2 * b + h]
                spread = jnp.concatenate(
                    [jnp.broadcast_to(s[0:1, i:i + 1], (1, QB)) for i in range(BLOCKS)], axis=1
                )
                q = quant[rows(2 * b + h), cols(p)].astype(jnp.float32)
                parts.append((q * spread).astype(jnp.bfloat16))
            w = jnp.concatenate(parts, axis=0)
            at = pl.ds(pl.multiple_of(b * 256, 256), 256)
            logits[at, :] += lax.dot_general(
                w, states[:, cols(p)], (((1,), (1,)), ((), ())), preferred_element_type=jnp.float32
            )

    step_own(0)
    step_own(1)

    @pl.loop(0, NP + 2)
    def _(k):
        @pl.when(k < NP - 2)
        def _():
            step_own(k + 2)

        @pl.when(k < NP)
        def _():
            step_near(k)

        @pl.when(jnp.logical_and(k >= 1, k < NP + 1))
        def _():
            step_far(k - 1)

        @pl.when(k == 2)
        def _():
            pltpu.make_async_copy(hidden, states, hid_sem).wait()

        @pl.when(k >= 2)
        def _():
            step_dot(k - 2)

    row = lax.broadcasted_iota(jnp.int32, (ROWS, QB), 0)

    @pl.loop(0, 8)
    def _(j):
        x = logits[:, pl.ds(pl.multiple_of(j * QB, QB), QB)]
        v = targets[pl.ds(j, 1), :]
        mine = lax.rem(v // QB, NT) == t
        column = jnp.where(mine, v // (NT * QB) * QB + lax.rem(v, QB), -1)
        top = jnp.max(x, axis=0, keepdims=True)
        total = jnp.sum(jnp.exp(x - top), axis=0, keepdims=True)
        stats[t, 0, pl.ds(j, 1), :] = top + jnp.log(total)
        stats[t, 1, pl.ds(j, 1), :] = jnp.sum(jnp.where(row == column, x, 0.0), axis=0, keepdims=True)

    @pl.loop(1, NT)
    def _(s):
        remote(stats.at[t], stats.at[t], st_send, st_recv, (g, lax.rem(t + s, NT)))

    lane = lax.broadcasted_iota(jnp.int32, (NG, QB), 1)
    table = jnp.zeros((NG, QB), jnp.float32)
    for p in range(NP):
        v = jnp.concatenate([scales[p, b, 0:1, :] for b in range(NG)], axis=0)
        v = pltpu.roll(v, p * BLOCKS, 1) if p else v
        table = jnp.where(jnp.logical_and(lane >= p * BLOCKS, lane < (p + 1) * BLOCKS), v, table)
    scale[...] = table[:, :NP * BLOCKS].astype(jnp.bfloat16)

    @pl.loop(1, NT)
    def _(s):
        wait(panel.at[:, tens(0)], a2a_send.at[lax.rem(t + s, NT)])

    @pl.loop(0, NP)
    def _(k):
        chunk = quant.at[rows(0), cols(0)]
        half = quant.at[rows(0, 0, HALF), cols(0)]
        for n in range(2):
            wait(chunk, own_send.at[n, k])
            wait(half, fwd_send.at[n, k])
        for n in range(4):
            wait(chunk, core_send.at[n, k])
        wait(scales.at[0, pl.ds(0, NG - 1)], sc_send.at[k])

    wait(stats.at[pl.ds(0, NT - 1)], st_recv)
    lses = stats[:, 0]
    top = jnp.max(lses, axis=0)
    lse = top + jnp.log(jnp.sum(jnp.exp(lses - top[None]), axis=0))
    picked = jnp.sum(stats[:, 1], axis=0)
    token = lax.broadcasted_iota(jnp.int32, (8, QB), 0) * QB + lax.broadcasted_iota(jnp.int32, (8, QB), 1)
    logprob[...] = jnp.where(token < counts[0], picked - lse, 0.0)
    wait(stats.at[pl.ds(0, NT - 1)], st_send)


def write(held, quant, sem):
    copies = [
        pltpu.make_async_copy(held.at[pl.ds(QB * i, QB)], quant.at[pl.ds(QB * i, QB)], sem.at[i]) for i in range(8)
    ]
    for copy in copies:
        copy.start()
    for copy in copies:
        copy.wait()


def local(panel, hidden, targets, counts):
    dma = pltpu.SemaphoreType.DMA
    vmem = pl.BlockSpec(memory_space=pltpu.VMEM)
    hbm = pl.BlockSpec(memory_space=pl.ANY)
    logprob, quant, scale = pl.pallas_call(
        kernel,
        out_shape=(
            jax.ShapeDtypeStruct((8, QB), jnp.float32),
            QUANT_SHAPE,
            jax.ShapeDtypeStruct((NG, NP * BLOCKS), jnp.bfloat16),
        ),
        in_specs=[hbm, hbm, vmem, pl.BlockSpec(memory_space=pltpu.SMEM)],
        out_specs=(vmem, vmem, vmem),
        scratch_shapes=[
            pltpu.VMEM((D, QB), jnp.bfloat16),
            pltpu.VMEM((ROWS, D), jnp.bfloat16),
            pltpu.VMEM((NP, NG, 8, QB), jnp.float32),
            pltpu.VMEM((ROWS, ROWS), jnp.float32),
            pltpu.VMEM((NT, 2, 8, QB), jnp.float32),
            dma((NT,)), dma((NT,)), dma(()),
            dma((2, NP)), dma((2, NP)), dma((4, NP)), dma((NP,)), dma(()),
            dma((NP,)), dma((NP,)), dma((NP,)), dma((NP,)), dma((4, NP)), dma((NP,)), dma(()),
        ],
        compiler_params=pltpu.CompilerParams(
            collective_id=0, has_side_effects=True, vmem_limit_bytes=VMEM_LIMIT
        ),
        cost_estimate=pl.CostEstimate(flops=2 * ROWS * ROWS * D, bytes_accessed=4 * ROWS * D, transcendentals=ROWS * ROWS),
        name="refresh",
    )(panel.T, hidden, targets.reshape(8, QB), counts)
    quant = pl.pallas_call(
        write,
        out_shape=pltpu.HBM((ROWS, D), jnp.bfloat16),
        in_specs=[vmem],
        out_specs=hbm,
        scratch_shapes=[dma((8,))],
        compiler_params=pltpu.CompilerParams(vmem_limit_bytes=2 << 20),
        cost_estimate=pl.CostEstimate(flops=0, bytes_accessed=4 * ROWS * D, transcendentals=0),
        name="write",
    )(quant)
    return logprob.reshape(ROWS), quant, scale


QUANT_SHAPE = pltpu.VMEM((ROWS, D), jnp.bfloat16)
VMEM_LIMIT = 32 << 20


def solution(mesh):
    in_specs = (P("group", "tensor"), P("group", None), P("group"), P("group"))
    out_specs = (P("group"), P("tensor", None), P("tensor", None))
    return jax.shard_map(local, mesh=mesh, in_specs=in_specs, out_specs=out_specs, check_vma=False)
```

time: 562 us -> 109 us (0.19)
  waiting for transfers between devices: 301 us -> 0 us
  Pallas kernels: 0 us -> 104 us
  local copies, waits for them, and re-layouts: 84 us -> 3.35 us
  blocking collectives: 73.4 us -> 0 us
  other arithmetic: 46.7 us -> 0 us
  matrix products: 34.1 us -> 0 us
  between operations: 14.7 us -> 1.3 us
  starting transfers between devices: 6.89 us -> 0 us
    all_to_all x1 -> x0, waiting for transfers between devices: 220 us -> none  [local(): lax.all_to_all(rows, 'tensor', split_axis=0, concat_axis=1, tiled=True)]
    pallas_call x0 -> x2, Pallas kernels: none -> 104 us  [the longest x1 99.1 us: local(): pl.pallas_call(kernel, out_shape=(jax.ShapeDtypeStruct((8, QB), jnp.float...]
    all_gather x1 -> x0, waiting for transfers between devices: 80.6 us -> none  [local(): rows = lax.all_gather(panel, 'group', axis=0, tiled=True)]
    unnamed x6, local copies, waits for them, and re-layouts: 42.8 us -> 3.35 us
    psum x1 -> x0, blocking collectives: 38 us -> none  [local(): total, target_logit = lax.psum((local_sum, picked), 'tensor')]
    pmax x1 -> x0, blocking collectives: 35.4 us -> none  [local(): top = lax.pmax(local_top, 'tensor')]
    dot_general x1 -> x0, matrix products: 34.1 us -> none  [local(): lax.dot_general(hidden, weights, (((1,), (1,)), ((), ())), preferred_elem...]
    convert_element_type x2 -> x0, other arithmetic: 23.4 us -> none  [the longest x1 23.4 us: quantize(): quant = (blocks / spread).astype(jnp.bfloat16)]
  transfers between devices with their start and end apart: 2 -> 0, of which waited for: 2 -> 0; matrix products, arithmetic and copies ran while one was open for 0% -> 0% of each run, Pallas kernels for 0% -> 0%
where the time goes in v1:
time: 109 us
  Pallas kernels  104 us (95%)
  local copies, waits for them, and re-layouts  3.35 us (3%)
  between operations  1.3 us (1%)
    pallas_call x1, Pallas kernels, local(): pl.pallas_call(kernel, out_shape=(jax.ShapeDtypeStruct((8, QB), jnp.float...  99.1 us
    pallas_call x1, Pallas kernels, local(): pl.pallas_call(write, out_shape=pltpu.HBM((ROWS, D), jnp.bfloat16), in_sp...  5.32 us
    unnamed x6, local copies, waits for them, and re-layouts  3.35 us

profile of v1, /device:TPU:0, one launch (start us, length us, event | category | flops | bytes accessed | tf_op | source)
XLA Modules:
  0.0 109.0 jit_solution(3228633385738726797)
XLA Ops:
  1.3 0.0 copy-start
  1.3 1.5 %copy-done = bf16[2048,448]{0,1:T(8,128)(2,1)S(1)} copy-done((bf16[2048,448]{0,1:T(8,128)(2,1)S(1)}, bf16[2048,448]{0,1:T(8,128)(2,1)}, u32[]{:S(2)}) %copy-start) | copy-done | bytes 1835032
  2.8 0.0 copy-start.1
  2.8 0.7 copy-done.1
  3.5 99.1 %refresh.1 = (f32[8,128]{1,0:T(8,128)S(1)}, bf16[1024,7168]{1,0:T(8,128)(2,1)S(1)}, bf16[8,56]{1,0:T(8,128)(2,1)S(1)}) custom-call(bf16[448,2048]{1,0:T(8,128)(2,1)S(1)} %bitcast.4, bf16[1024,7168]{1,0:T(8,128)(2,1)} %hidden.1, s32[8,128]{1,0:T(8,128)S(1)} %bitcast.5, s32[1]{0:T(128)S(6)} %copy.9.counts), custom_call_target="tpu_custom_call" | custom-call | flops 15032385536 | bytes 29360128 | tf_op jit(solution)/shard_map/refresh/pallas_call | solution.py:247
  102.5 5.3 %write.1 = bf16[1024,7168]{1,0:T(8,128)(2,1)} custom-call(bf16[1024,7168]{1,0:T(8,128)(2,1)S(1)} %get-tuple-element.7.held), custom_call_target="tpu_custom_call" | custom-call | bytes 29360128 | tf_op jit(solution)/shard_map/write/pallas_call | solution.py:272
  107.9 0.6 copy.10
  108.5 0.6 copy.11
Async XLA Ops:
  1.3 1.5 %copy-start = (bf16[2048,448]{0,1:T(8,128)(2,1)S(1)}, bf16[2048,448]{0,1:T(8,128)(2,1)}, u32[]{:S(2)}) copy-start(bf16[2048,448]{0,1:T(8,128)(2,1)} %param.4) | copy-start | bytes 5505028
  2.8 0.7 copy-start.1

commit v2 on v1

v2 whole, which is shorter than its diff:
```python
import functools

import jax
import jax.numpy as jnp
from jax import lax
from jax.experimental import pallas as pl
from jax.experimental.pallas import tpu as pltpu
from jax.sharding import PartitionSpec as P

MESH = pl.DeviceIdType.MESH
QB = 128
NZ = 4
NG = 8
NT = 16
NP = 8
ROWS = 1024
D = 7168
SRC = D // NT
CW = 2 * SRC
BLOCKS = CW // QB
HALF = QB // 2
LEAD = 2
AHEAD = 4
LAG = 2
VMEM_LIMIT = 32 << 20


def kernel(
    panel, hidden, targets, counts,
    logprob, quant, scale,
    arrived, states, scales, logits, wanted, parts, stats,
    a2a_send, a2a_recv, hid_sem, tgt_sem,
    own_send, fwd_send, core_send, sc_send, st_send,
    prev_recv, next_recv, top_recv, bot_recv, core_recv, sc_recv, st_recv,
):
    g = lax.axis_index("group")
    t = lax.axis_index("tensor")
    z, c = g // 2, lax.rem(g, 2)
    gp = lax.rem(z + 3, NZ) * 2 + c
    gn = lax.rem(z + 1, NZ) * 2 + c
    gf = lax.rem(z + 2, NZ) * 2 + c
    go = z * 2 + 1 - c
    y, xh, odd = t // 4, lax.rem(t, 4) // 2, lax.rem(t, 2)

    def shift(k):
        between = jnp.logical_and(k >= 2, k < 6)
        odd_step = lax.rem(k, 2)
        return jnp.where(between, 1 + 2 * odd_step, k // 6 * 2), jnp.where(between, k // 4, odd_step)

    def pair(k):
        dy, dx = shift(k)
        return lax.rem(y + dy, 4) * 2 + lax.rem(xh + dx, 2)

    def cols(p):
        return pl.ds(pl.multiple_of(p * CW, CW), CW)

    def rows(b, first=0, size=QB):
        return pl.ds(pl.multiple_of(b * QB + first, HALF), size)

    def tens(u):
        return pl.ds(pl.multiple_of(u * QB, QB), QB)

    def block_of(u):
        return pl.ds(pl.multiple_of(u * SRC, SRC), SRC)

    def wait(ref, sem):
        pltpu.make_async_copy(ref, ref, sem).wait()

    def remote(src, dst, send, recv, to):
        pltpu.make_async_remote_copy(
            src_ref=src, dst_ref=dst, send_sem=send, recv_sem=recv, device_id=to, device_id_type=MESH
        ).start()

    pltpu.make_async_copy(panel.at[:, tens(t)], arrived.at[block_of(t)], a2a_recv.at[t]).start()
    barrier = pltpu.get_barrier_semaphore()

    @pl.loop(1, NT)
    def _(s):
        pl.semaphore_signal(barrier, inc=1, device_id=(g, lax.rem(t + s, NT)), device_id_type=MESH)

    @pl.loop(1, NG)
    def _(s):
        pl.semaphore_signal(barrier, inc=1, device_id=(lax.rem(g + s, NG), t), device_id_type=MESH)

    pltpu.make_async_copy(targets, wanted, tgt_sem).start()

    def batch(k):
        return k // 2

    def quantize(k, first, count):
        p, e = pair(k), batch(k)
        lane = lax.broadcasted_iota(jnp.int32, (8, QB), 1)
        tile = scales[e, g]
        for i in range(count):
            at = pl.multiple_of(p * CW + (first + i) * QB, QB)
            block = arrived[pl.ds(at, QB)].astype(jnp.float32)
            largest = jnp.max(jnp.abs(block), axis=(0, 1), keepdims=True)
            s = ((largest + 1e-06) / 448.0).astype(jnp.bfloat16).astype(jnp.float32)
            quant[rows(g), pl.ds(at, QB)] = (block / s).astype(jnp.bfloat16).T
            tile = jnp.where(lane == p * BLOCKS + first + i, jnp.broadcast_to(s, (8, QB)), tile)
        scales[e, g] = tile

    def send_own(k, at, width):
        block = quant.at[rows(g), pl.ds(pl.multiple_of(at, QB), width)]
        remote(block, block, own_send.at[0, k], prev_recv.at[k], (gn, t))
        remote(block, block, own_send.at[1, k], next_recv.at[k], (gp, t))
        remote(block, block, core_send.at[0, k], core_recv.at[0, k], (go, t))

    def send_scales(e):
        @pl.loop(1, NG)
        def _(s):
            remote(scales.at[e, g], scales.at[e, g], sc_send.at[e], sc_recv.at[e], (lax.rem(g + s, NG), t))

    p0 = pair(0)
    first = 4 * odd
    wait(arrived.at[block_of(t)], a2a_recv.at[t])
    for e in range(NP // 2):
        scales[e, g] = jnp.zeros((8, QB), jnp.float32)
    quantize(0, first, 3)
    logits[...] = jnp.zeros_like(logits)

    pl.semaphore_wait(barrier, NT - 1 + NG - 1)

    def send_block(u):
        remote(panel.at[:, tens(u)], arrived.at[block_of(t)], a2a_send.at[u], a2a_recv.at[t], (g, u))

    def send_pair(j):
        dy, dx = shift(j)
        q = lax.rem(y + 4 - dy, 4) * 2 + lax.rem(xh + dx, 2)
        send_block(2 * q)
        send_block(2 * q + 1)

    send_block(2 * p0 + 1 - odd)
    send_own(0, p0 * CW + first * QB, 3 * QB)
    for j in range(1, AHEAD):
        send_pair(j)
    pltpu.make_async_copy(hidden, states, hid_sem).start()

    other = 2 * p0 + 1 - odd
    wait(arrived.at[block_of(other)], a2a_recv.at[other])
    first = 3 - 3 * odd
    quantize(0, first, 4)
    send_own(0, p0 * CW + first * QB, 4 * QB)

    def step_own(k):
        p = pair(k)
        wait(arrived.at[block_of(2 * p)], a2a_recv.at[2 * p])
        wait(arrived.at[block_of(2 * p + 1)], a2a_recv.at[2 * p + 1])
        quantize(k, 0, BLOCKS)

        @pl.when(lax.rem(k, 2) == 1)
        def _():
            send_scales(batch(k))

        send_own(k, p * CW, CW)

    def step_near(k):
        p = pair(k)
        block = quant.at[rows(gp), cols(p)]
        wait(block, prev_recv.at[k])
        top = quant.at[rows(gp, 0, HALF), cols(p)]
        remote(top, top, fwd_send.at[0, k], top_recv.at[k], (gn, t))
        remote(block, block, core_send.at[1, k], core_recv.at[1, k], (go, t))
        block = quant.at[rows(gn), cols(p)]
        wait(block, next_recv.at[k])
        bot = quant.at[rows(gn, HALF, HALF), cols(p)]
        remote(bot, bot, fwd_send.at[1, k], bot_recv.at[k], (gp, t))
        remote(block, block, core_send.at[2, k], core_recv.at[2, k], (go, t))

    def step_far(k):
        p = pair(k)
        wait(quant.at[rows(gf, 0, HALF), cols(p)], top_recv.at[k])
        wait(quant.at[rows(gf, HALF, HALF), cols(p)], bot_recv.at[k])
        block = quant.at[rows(gf), cols(p)]
        remote(block, block, core_send.at[3, k], core_recv.at[3, k], (go, t))

    def dot(k, b):
        p = pair(k)
        both = []
        for h in range(2):
            s = pltpu.roll(scales[batch(k), 2 * b + h], lax.rem(QB - p * BLOCKS, QB), 1)
            spread = jnp.concatenate([jnp.broadcast_to(s[0:1, i:i + 1], (1, QB)) for i in range(BLOCKS)], axis=1)
            q = quant[rows(2 * b + h), cols(p)].astype(jnp.float32)
            both.append((q * spread).astype(jnp.bfloat16))
        w = jnp.concatenate(both, axis=0)
        at = pl.ds(pl.multiple_of(b * 256, 256), 256)
        logits[at, :] += lax.dot_general(
            w, states[:, cols(p)], (((1,), (1,)), ((), ())), preferred_element_type=jnp.float32
        )

    def dot_near(k):
        p = pair(k)
        for n in range(3):
            wait(quant.at[rows(0), cols(p)], core_recv.at[n, k])

        @pl.loop(0, 3)
        def _(j):
            dot(k, lax.rem(z + 3 + j, NZ))

    def dot_far(k):
        p = pair(k)
        wait(quant.at[rows(0), cols(p)], core_recv.at[3, k])
        dot(k, lax.rem(z + 2, NZ))

    for k in range(1, LEAD):
        send_pair(AHEAD - 1 + k)
        step_own(jnp.int32(k))

    @pl.loop(0, NP)
    def _(k):
        @pl.when(k < NP - (AHEAD - 1 + LEAD))
        def _():
            send_pair(k + AHEAD - 1 + LEAD)

        @pl.when(k < NP - LEAD)
        def _():
            step_own(k + LEAD)

        step_near(k)

        @pl.when(k >= LAG)
        def _():
            step_far(k - LAG)

        @pl.when(k == 0)
        def _():
            pltpu.make_async_copy(hidden, states, hid_sem).wait()

        @pl.when(lax.rem(k, 2) == 0)
        def _():
            wait(scales.at[0, pl.ds(0, NG - 1)], sc_recv.at[batch(k)])

        @pl.when(k < NP - 1)
        def _():
            dot_near(k)

        @pl.when(k >= LAG)
        def _():
            dot_far(k - LAG)

    row = lax.broadcasted_iota(jnp.int32, (256, QB), 0)
    pltpu.make_async_copy(targets, wanted, tgt_sem).wait()

    def measure(b):
        @pl.loop(0, 8, unroll=4)
        def _(j):
            x = logits[pl.ds(pl.multiple_of(b * 256, 256), 256), pl.ds(pl.multiple_of(j * QB, QB), QB)]
            v = wanted[pl.ds(j, 1), :]
            mine = lax.rem(v // QB, NT) == t
            column = jnp.where(mine, v // (NT * QB) * QB + lax.rem(v, QB) - b * 256, -1)
            top = jnp.max(x, axis=0, keepdims=True)
            total = jnp.sum(jnp.exp(x - top), axis=0, keepdims=True)
            parts[b, 0, pl.ds(j, 1), :] = top + jnp.log(total)
            parts[b, 1, pl.ds(j, 1), :] = jnp.sum(jnp.where(row == column, x, 0.0), axis=0, keepdims=True)

    def combine(lses):
        top = jnp.max(lses, axis=0)
        return top + jnp.log(jnp.sum(jnp.exp(lses - top[None]), axis=0))

    for k in range(NP - LAG, NP):
        if k == NP - 1:
            @pl.loop(0, 3)
            def _(j):
                measure(lax.rem(z + 3 + j, NZ))

        step_far(k)
        if k == NP - LAG:
            dot_near(NP - 1)
        dot_far(k)

    measure(lax.rem(z + 2, NZ))
    stats[t, 0] = combine(parts[:, 0])
    stats[t, 1] = jnp.sum(parts[:, 1], axis=0)

    @pl.loop(1, NT)
    def _(s):
        remote(stats.at[t], stats.at[t], st_send, st_recv, (g, lax.rem(t + s, NT)))

    table = jnp.concatenate([jnp.sum(scales[:, b, 0:1, :], axis=0) for b in range(NG)], axis=0)
    scale[...] = table[:, :NP * BLOCKS].astype(jnp.bfloat16)

    @pl.loop(1, NT)
    def _(s):
        wait(panel.at[:, tens(0)], a2a_send.at[lax.rem(t + s, NT)])

    @pl.loop(0, NP)
    def _(k):
        chunk = quant.at[rows(0), cols(0)]
        half = quant.at[rows(0, 0, HALF), cols(0)]
        for n in range(2):
            wait(chunk, own_send.at[n, k])
            wait(half, fwd_send.at[n, k])
        for n in range(4):
            wait(chunk, core_send.at[n, k])

    for e in range(NP // 2):
        wait(scales.at[0, pl.ds(0, NG - 1)], sc_send.at[e])

    wait(stats.at[pl.ds(0, NT - 1)], st_recv)
    token = lax.broadcasted_iota(jnp.int32, (8, QB), 0) * QB + lax.broadcasted_iota(jnp.int32, (8, QB), 1)
    gap = jnp.sum(stats[:, 1], axis=0) - combine(stats[:, 0])
    logprob[...] = jnp.where(token < counts[0], gap, 0.0)
    wait(stats.at[pl.ds(0, NT - 1)], st_send)


def write(held, held_logprob, held_scale, quant, logprob, scale, sem):
    copies = [
        pltpu.make_async_copy(held.at[pl.ds(QB * i, QB)], quant.at[pl.ds(QB * i, QB)], sem.at[i]) for i in range(8)
    ]
    copies.append(pltpu.make_async_copy(held_logprob, logprob, sem.at[8]))
    copies.append(pltpu.make_async_copy(held_scale, scale, sem.at[9]))
    for copy in copies:
        copy.start()
    for copy in copies:
        copy.wait()


def local(panel, hidden, targets, counts):
    dma = pltpu.SemaphoreType.DMA
    vmem = pl.BlockSpec(memory_space=pltpu.VMEM)
    hbm = pl.BlockSpec(memory_space=pltpu.HBM)
    held = pl.pallas_call(
        kernel,
        out_shape=(
            pltpu.VMEM((8, QB), jnp.float32),
            pltpu.VMEM((ROWS, D), jnp.bfloat16),
            pltpu.VMEM((NG, NP * BLOCKS), jnp.bfloat16),
        ),
        in_specs=[hbm, hbm, hbm, pl.BlockSpec(memory_space=pltpu.SMEM)],
        out_specs=(vmem, vmem, vmem),
        scratch_shapes=[
            pltpu.VMEM((D, QB), jnp.bfloat16),
            pltpu.VMEM((ROWS, D), jnp.bfloat16),
            pltpu.VMEM((NP // 2, NG, 8, QB), jnp.float32),
            pltpu.VMEM((ROWS, ROWS), jnp.float32),
            pltpu.VMEM((8, QB), jnp.int32),
            pltpu.VMEM((NZ, 2, 8, QB), jnp.float32),
            pltpu.VMEM((NT, 2, 8, QB), jnp.float32),
            dma((NT,)), dma((NT,)), dma(()), dma(()),
            dma((2, NP)), dma((2, NP)), dma((4, NP)), dma((NP // 2,)), dma(()),
            dma((NP,)), dma((NP,)), dma((NP,)), dma((NP,)), dma((4, NP)), dma((NP // 2,)), dma(()),
        ],
        compiler_params=pltpu.CompilerParams(
            collective_id=0, has_side_effects=True, vmem_limit_bytes=VMEM_LIMIT
        ),
        cost_estimate=pl.CostEstimate(
            flops=2 * ROWS * ROWS * D, bytes_accessed=4 * ROWS * D, transcendentals=ROWS * ROWS
        ),
        name="refresh",
    )(
        pltpu.with_memory_space_constraint(panel.T, pltpu.HBM),
        hidden,
        pltpu.with_memory_space_constraint(targets.reshape(8, QB), pltpu.HBM),
        counts,
    )
    quant, logprob, scale = pl.pallas_call(
        write,
        out_shape=(
            pltpu.HBM((ROWS, D), jnp.bfloat16),
            pltpu.HBM((8, QB), jnp.float32),
            pltpu.HBM((NG, NP * BLOCKS), jnp.bfloat16),
        ),
        in_specs=[vmem] * 3,
        out_specs=(hbm,) * 3,
        scratch_shapes=[dma((10,))],
        compiler_params=pltpu.CompilerParams(vmem_limit_bytes=2 << 20),
        cost_estimate=pl.CostEstimate(flops=0, bytes_accessed=4 * ROWS * D, transcendentals=0),
        name="write",
    )(held[1], held[0], held[2])
    return logprob.reshape(ROWS), quant, scale


def solution(mesh):
    in_specs = (P("group", "tensor"), P("group", None), P("group"), P("group"))
    out_specs = (P("group"), P("tensor", None), P("tensor", None))
    return jax.shard_map(local, mesh=mesh, in_specs=in_specs, out_specs=out_specs, check_vma=False)
```

time: 109 us -> 93.1 us (0.85)
  Pallas kernels: 104 us -> 91.6 us
  local copies, waits for them, and re-layouts: 3.35 us -> 0 us
    pallas_call x2, Pallas kernels: 104 us -> 91.6 us  [the longest x1 86.3 us: local(): pl.pallas_call(kernel, out_shape=(pltpu.VMEM((8, QB), jnp.float32), pltpu...]
    unnamed x6 -> x0, local copies, waits for them, and re-layouts: 3.35 us -> none
where the time goes in v2:
time: 93.1 us; the launch traced here: 92.9 us
  Pallas kernels  91.6 us (98%)
  between operations  1.29 us (1%)
    pallas_call x1, Pallas kernels, local(): pl.pallas_call(kernel, out_shape=(pltpu.VMEM((8, QB), jnp.float32), pltpu...  86.3 us
    pallas_call x1, Pallas kernels, local(): pl.pallas_call(write, out_shape=(pltpu.HBM((ROWS, D), jnp.bfloat16), pltp...  5.34 us

profile of v2, /device:TPU:0, one launch (start us, length us, event | category | flops | bytes accessed | tf_op | source)
XLA Modules:
  0.0 92.9 jit_solution(578714585771839176)
XLA Ops:
  1.3 86.3 %refresh.1 = (f32[8,128]{1,0:T(8,128)S(1)}, bf16[1024,7168]{1,0:T(8,128)(2,1)S(1)}, bf16[8,56]{1,0:T(8,128)(2,1)S(1)}) custom-call(bf16[448,2048]{1,0:T(8,128)(2,1)} %bitcast.3, bf16[1024,7168]{1,0:T(8,128)(2,1)} %hidden.1, s32[8,128]{1,0:T(8,128)} %bitcast.4, s32[1]{0:T(128)S(6)} %copy.7.counts), custom_call_target="tpu_custom_call" | custom-call | flops 15032385536 | bytes 29360128 | tf_op jit(solution)/shard_map/refresh/pallas_call | solution.py:322
  87.6 5.3 %write.1 = (bf16[1024,7168]{1,0:T(8,128)(2,1)}, f32[8,128]{1,0:T(8,128)}, bf16[8,56]{1,0:T(8,128)(2,1)}) custom-call(bf16[1024,7168]{1,0:T(8,128)(2,1)S(1)} %get-tuple-element.9.held, f32[8,128]{1,0:T(8,128)S(1)} %get-tuple-element.10.held_logprob, bf16[8,56]{1,0:T(8,128)(2,1)S(1)} %get-tuple-element.11.held_scale), custom_call_target="tpu_custom_call" | custom-call | bytes 29360128 | tf_op jit(solution)/shard_map/write/pallas_call | solution.py:356

commit v3 on v2

--- a/solution.py
+++ b/solution.py
@@ -29,7 +29,7 @@
     panel, hidden, targets, counts,
     logprob, quant, scale,
     arrived, states, scales, logits, wanted, parts, stats,
-    a2a_send, a2a_recv, hid_sem, tgt_sem,
+    a2a_send, a2a_recv, hid_sem, tgt_sem, near_recv, near_send,
     own_send, fwd_send, core_send, sc_send, st_send,
     prev_recv, next_recv, top_recv, bot_recv, core_recv, sc_recv, st_recv,
 ):
@@ -43,9 +43,8 @@
     y, xh, odd = t // 4, lax.rem(t, 4) // 2, lax.rem(t, 2)
 
     def shift(k):
-        between = jnp.logical_and(k >= 2, k < 6)
-        odd_step = lax.rem(k, 2)
-        return jnp.where(between, 1 + 2 * odd_step, k // 6 * 2), jnp.where(between, k // 4, odd_step)
+        r = lax.rem(k, 3)
+        return jnp.where(k < 6, r + r // 2, 2), jnp.where(k < 6, k // 3, k - 6)
 
     def pair(k):
         dy, dx = shift(k)
@@ -73,6 +72,7 @@
 
     pltpu.make_async_copy(panel.at[:, tens(t)], arrived.at[block_of(t)], a2a_recv.at[t]).start()
     barrier = pltpu.get_barrier_semaphore()
+    p0 = pair(0)
 
     @pl.loop(1, NT)
     def _(s):
@@ -89,7 +89,7 @@
 
     def quantize(k, first, count):
         p, e = pair(k), batch(k)
-        lane = lax.broadcasted_iota(jnp.int32, (8, QB), 1)
+        lane = lax.broadcasted_iota(jnp.int32, (1, QB), 1)
         tile = scales[e, g]
         for i in range(count):
             at = pl.multiple_of(p * CW + (first + i) * QB, QB)
@@ -97,7 +97,7 @@
             largest = jnp.max(jnp.abs(block), axis=(0, 1), keepdims=True)
             s = ((largest + 1e-06) / 448.0).astype(jnp.bfloat16).astype(jnp.float32)
             quant[rows(g), pl.ds(at, QB)] = (block / s).astype(jnp.bfloat16).T
-            tile = jnp.where(lane == p * BLOCKS + first + i, jnp.broadcast_to(s, (8, QB)), tile)
+            tile = jnp.where(lane == p * BLOCKS + first + i, jnp.broadcast_to(s, (1, QB)), tile)
         scales[e, g] = tile
 
     def send_own(k, at, width):
@@ -111,14 +111,6 @@
         def _(s):
             remote(scales.at[e, g], scales.at[e, g], sc_send.at[e], sc_recv.at[e], (lax.rem(g + s, NG), t))
 
-    p0 = pair(0)
-    first = 4 * odd
-    wait(arrived.at[block_of(t)], a2a_recv.at[t])
-    for e in range(NP // 2):
-        scales[e, g] = jnp.zeros((8, QB), jnp.float32)
-    quantize(0, first, 3)
-    logits[...] = jnp.zeros_like(logits)
-
     pl.semaphore_wait(barrier, NT - 1 + NG - 1)
 
     def send_block(u):
@@ -130,17 +122,42 @@
         send_block(2 * q)
         send_block(2 * q + 1)
 
-    send_block(2 * p0 + 1 - odd)
-    send_own(0, p0 * CW + first * QB, 3 * QB)
+    other = 2 * p0 + 1 - odd
+    edge = HALF + QB
+
+    def columns(u, at, size):
+        return pl.ds(pl.multiple_of(u * SRC + at, HALF), size)
+
+    def near_part(u, side, first):
+        at = (SRC - edge) * (1 - side) if first else edge * side
+        return at, (edge if first else SRC - edge)
+
+    for part in (True, False):
+        at, size = near_part(t, odd, part)
+        remote(
+            panel.at[pl.ds(pl.multiple_of(at, HALF), size), tens(other)],
+            arrived.at[columns(t, at, size)],
+            near_send if part else a2a_send.at[other],
+            near_recv if part else a2a_recv.at[t],
+            (g, other),
+        )
+
+    for e in range(NP // 2):
+        scales[e, g] = jnp.zeros((1, QB), jnp.float32)
+    wait(arrived.at[block_of(t)], a2a_recv.at[t])
+    quantize(0, 4 * odd, 3)
+    send_own(0, p0 * CW + 4 * odd * QB, 3 * QB)
     for j in range(1, AHEAD):
         send_pair(j)
     pltpu.make_async_copy(hidden, states, hid_sem).start()
-
-    other = 2 * p0 + 1 - odd
-    wait(arrived.at[block_of(other)], a2a_recv.at[other])
-    first = 3 - 3 * odd
-    quantize(0, first, 4)
-    send_own(0, p0 * CW + first * QB, 4 * QB)
+    logits[...] = jnp.zeros_like(logits)
+
+    for part in (True, False):
+        at, size = near_part(other, 1 - odd, part)
+        wait(arrived.at[columns(other, at, size)], near_recv if part else a2a_recv.at[other])
+        first = (3 - 1 * odd) if part else (5 - 5 * odd)
+        quantize(0, first, 2)
+        send_own(0, p0 * CW + first * QB, 2 * QB)
 
     def step_own(k):
         p = pair(k)
@@ -202,9 +219,15 @@
         wait(quant.at[rows(0), cols(p)], core_recv.at[3, k])
         dot(k, lax.rem(z + 2, NZ))
 
-    for k in range(1, LEAD):
-        send_pair(AHEAD - 1 + k)
-        step_own(jnp.int32(k))
+    p1 = pair(1)
+    for first, count in ((0, 3), (3, 4)):
+        source = 2 * p1 + first // 3
+        wait(arrived.at[block_of(source)], a2a_recv.at[source])
+        quantize(1, first, count)
+        if first:
+            send_scales(0)
+        send_own(1, p1 * CW + first * QB, count * QB)
+    send_pair(AHEAD)
 
     @pl.loop(0, NP)
     def _(k):
@@ -218,24 +241,19 @@
 
         step_near(k)
 
+        @pl.when(k == 0)
+        def _():
+            pltpu.make_async_copy(hidden, states, hid_sem).wait()
+
+        @pl.when(lax.rem(k, 2) == 0)
+        def _():
+            wait(scales.at[0, pl.ds(0, NG - 1)], sc_recv.at[batch(k)])
+
+        dot_near(k)
+
         @pl.when(k >= LAG)
         def _():
             step_far(k - LAG)
-
-        @pl.when(k == 0)
-        def _():
-            pltpu.make_async_copy(hidden, states, hid_sem).wait()
-
-        @pl.when(lax.rem(k, 2) == 0)
-        def _():
-            wait(scales.at[0, pl.ds(0, NG - 1)], sc_recv.at[batch(k)])
-
-        @pl.when(k < NP - 1)
-        def _():
-            dot_near(k)
-
-        @pl.when(k >= LAG)
-        def _():
             dot_far(k - LAG)
 
     row = lax.broadcasted_iota(jnp.int32, (256, QB), 0)
@@ -257,17 +275,15 @@
         top = jnp.max(lses, axis=0)
         return top + jnp.log(jnp.sum(jnp.exp(lses - top[None]), axis=0))
 
-    for k in range(NP - LAG, NP):
-        if k == NP - 1:
-            @pl.loop(0, 3)
-            def _(j):
-                measure(lax.rem(z + 3 + j, NZ))
-
-        step_far(k)
-        if k == NP - LAG:
-            dot_near(NP - 1)
-        dot_far(k)
-
+    step_far(NP - 2)
+
+    @pl.loop(0, 3)
+    def _(j):
+        measure(lax.rem(z + 3 + j, NZ))
+
+    step_far(NP - 1)
+    dot_far(NP - 2)
+    dot_far(NP - 1)
     measure(lax.rem(z + 2, NZ))
     stats[t, 0] = combine(parts[:, 0])
     stats[t, 1] = jnp.sum(parts[:, 1], axis=0)
@@ -276,12 +292,17 @@
     def _(s):
         remote(stats.at[t], stats.at[t], st_send, st_recv, (g, lax.rem(t + s, NT)))
 
-    table = jnp.concatenate([jnp.sum(scales[:, b, 0:1, :], axis=0) for b in range(NG)], axis=0)
+    table = jnp.concatenate([jnp.sum(scales[:, b], axis=0) for b in range(NG)], axis=0)
     scale[...] = table[:, :NP * BLOCKS].astype(jnp.bfloat16)
 
-    @pl.loop(1, NT)
-    def _(s):
-        wait(panel.at[:, tens(0)], a2a_send.at[lax.rem(t + s, NT)])
+    wait(panel.at[pl.ds(0, edge), tens(0)], near_send)
+    wait(panel.at[pl.ds(0, SRC - edge), tens(0)], a2a_send.at[other])
+
+    @pl.loop(1, NP)
+    def _(j):
+        q = lax.rem(p0 + j, NP)
+        wait(panel.at[:, tens(0)], a2a_send.at[2 * q])
+        wait(panel.at[:, tens(0)], a2a_send.at[2 * q + 1])
 
     @pl.loop(0, NP)
     def _(k):
@@ -331,12 +352,12 @@
         scratch_shapes=[
             pltpu.VMEM((D, QB), jnp.bfloat16),
             pltpu.VMEM((ROWS, D), jnp.bfloat16),
-            pltpu.VMEM((NP // 2, NG, 8, QB), jnp.float32),
+            pltpu.VMEM((NP // 2, NG, 1, QB), jnp.float32),
             pltpu.VMEM((ROWS, ROWS), jnp.float32),
             pltpu.VMEM((8, QB), jnp.int32),
             pltpu.VMEM((NZ, 2, 8, QB), jnp.float32),
             pltpu.VMEM((NT, 2, 8, QB), jnp.float32),
-            dma((NT,)), dma((NT,)), dma(()), dma(()),
+            dma((NT,)), dma((NT,)), dma(()), dma(()), dma(()), dma(()),
             dma((2, NP)), dma((2, NP)), dma((4, NP)), dma((NP // 2,)), dma(()),
             dma((NP,)), dma((NP,)), dma((NP,)), dma((NP,)), dma((4, NP)), dma((NP // 2,)), dma(()),
         ],

time: 93.1 us -> 90 us (0.967)
  Pallas kernels: 91.6 us -> 88.3 us
    pallas_call x1, Pallas kernels: 86.3 us -> 83 us  [local(): pl.pallas_call(kernel, out_shape=(pltpu.VMEM((8, QB), jnp.float32), pltpu...]
where the time goes in v3:
time: 90 us; the launch traced here: 89.6 us
  Pallas kernels  88.3 us (98%)
  between operations  1.29 us (1%)
    pallas_call x1, Pallas kernels, local(): pl.pallas_call(kernel, out_shape=(pltpu.VMEM((8, QB), jnp.float32), pltpu...  83 us
    pallas_call x1, Pallas kernels, local(): pl.pallas_call(write, out_shape=(pltpu.HBM((ROWS, D), jnp.bfloat16), pltp...  5.34 us

profile of v3, /device:TPU:0, one launch (start us, length us, event | category | flops | bytes accessed | tf_op | source)
XLA Modules:
  0.0 89.6 jit_solution(466714803939354910)
XLA Ops:
  1.3 83.0 %refresh.1 = (f32[8,128]{1,0:T(8,128)S(1)}, bf16[1024,7168]{1,0:T(8,128)(2,1)S(1)}, bf16[8,56]{1,0:T(8,128)(2,1)S(1)}) custom-call(bf16[448,2048]{1,0:T(8,128)(2,1)} %bitcast.3, bf16[1024,7168]{1,0:T(8,128)(2,1)} %hidden.1, s32[8,128]{1,0:T(8,128)} %bitcast.4, s32[1]{0:T(128)S(6)} %copy.7.counts), custom_call_target="tpu_custom_call" | custom-call | flops 15032385536 | bytes 29360128 | tf_op jit(solution)/shard_map/refresh/pallas_call | solution.py:343
  84.3 5.3 %write.1 = (bf16[1024,7168]{1,0:T(8,128)(2,1)}, f32[8,128]{1,0:T(8,128)}, bf16[8,56]{1,0:T(8,128)(2,1)}) custom-call(bf16[1024,7168]{1,0:T(8,128)(2,1)S(1)} %get-tuple-element.9.held, f32[8,128]{1,0:T(8,128)S(1)} %get-tuple-element.10.held_logprob, bf16[8,56]{1,0:T(8,128)(2,1)S(1)} %get-tuple-element.11.held_scale), custom_call_target="tpu_custom_call" | custom-call | bytes 29360128 | tf_op jit(solution)/shard_map/write/pallas_call | solution.py:377

commit v4 on v3

--- a/solution.py
+++ b/solution.py
@@ -43,8 +43,11 @@
     y, xh, odd = t // 4, lax.rem(t, 4) // 2, lax.rem(t, 2)
 
     def shift(k):
-        r = lax.rem(k, 3)
-        return jnp.where(k < 6, r + r // 2, 2), jnp.where(k < 6, k // 3, k - 6)
+        def among(*steps):
+            return functools.reduce(jnp.logical_or, [k == n for n in steps])
+
+        dy = jnp.where(among(1, 4), 1, jnp.where(among(3, 5), 3, jnp.where(k >= 6, 2, 0)))
+        return dy, jnp.where(among(2, 4, 5, 7), 1, 0)
 
     def pair(k):
         dy, dx = shift(k)
@@ -205,18 +208,20 @@
             w, states[:, cols(p)], (((1,), (1,)), ((), ())), preferred_element_type=jnp.float32
         )
 
+    def dot_own(k):
+        wait(quant.at[rows(0), cols(0)], core_recv.at[0, k])
+        dot(k, z)
+
     def dot_near(k):
-        p = pair(k)
-        for n in range(3):
-            wait(quant.at[rows(0), cols(p)], core_recv.at[n, k])
-
-        @pl.loop(0, 3)
+        for n in range(1, 3):
+            wait(quant.at[rows(0), cols(0)], core_recv.at[n, k])
+
+        @pl.loop(0, 2)
         def _(j):
-            dot(k, lax.rem(z + 3 + j, NZ))
+            dot(k, lax.rem(z + 1 + 2 * j, NZ))
 
     def dot_far(k):
-        p = pair(k)
-        wait(quant.at[rows(0), cols(p)], core_recv.at[3, k])
+        wait(quant.at[rows(0), cols(0)], core_recv.at[3, k])
         dot(k, lax.rem(z + 2, NZ))
 
     p1 = pair(1)
@@ -228,6 +233,9 @@
             send_scales(0)
         send_own(1, p1 * CW + first * QB, count * QB)
     send_pair(AHEAD)
+    for k in range(2, LEAD):
+        send_pair(AHEAD - 1 + k)
+        step_own(jnp.int32(k))
 
     @pl.loop(0, NP)
     def _(k):
@@ -239,8 +247,16 @@
         def _():
             step_own(k + LEAD)
 
+        @pl.when(lax.rem(k, 2) == 1)
+        def _():
+            dot_own(k)
+
         step_near(k)
 
+        @pl.when(k >= LAG)
+        def _():
+            step_far(k - LAG)
+
         @pl.when(k == 0)
         def _():
             pltpu.make_async_copy(hidden, states, hid_sem).wait()
@@ -248,12 +264,12 @@
         @pl.when(lax.rem(k, 2) == 0)
         def _():
             wait(scales.at[0, pl.ds(0, NG - 1)], sc_recv.at[batch(k)])
+            dot_own(k)
 
         dot_near(k)
 
         @pl.when(k >= LAG)
         def _():
-            step_far(k - LAG)
             dot_far(k - LAG)
 
     row = lax.broadcasted_iota(jnp.int32, (256, QB), 0)
@@ -274,6 +290,10 @@
     def combine(lses):
         top = jnp.max(lses, axis=0)
         return top + jnp.log(jnp.sum(jnp.exp(lses - top[None]), axis=0))
+
+    for k in range(NP - LAG, NP - 2):
+        step_far(k)
+        dot_far(k)
 
     step_far(NP - 2)
 

time: 90 us -> 88.8 us (0.987)
  Pallas kernels: 88.3 us -> 86.3 us
    pallas_call x1, Pallas kernels: 83 us -> 81 us  [local(): pl.pallas_call(kernel, out_shape=(pltpu.VMEM((8, QB), jnp.float32), pltpu...]
where the time goes in v4:
time: 88.8 us; the launch traced here: 87.6 us
  Pallas kernels  86.3 us (97%)
  between operations  1.29 us (1%)
    pallas_call x1, Pallas kernels, local(): pl.pallas_call(kernel, out_shape=(pltpu.VMEM((8, QB), jnp.float32), pltpu...  81 us
    pallas_call x1, Pallas kernels, local(): pl.pallas_call(write, out_shape=(pltpu.HBM((ROWS, D), jnp.bfloat16), pltp...  5.34 us

profile of v4, /device:TPU:0, one launch (start us, length us, event | category | flops | bytes accessed | tf_op | source)
XLA Modules:
  0.0 87.6 jit_solution(17200251011596265493)
XLA Ops:
  1.3 81.0 %refresh.1 = (f32[8,128]{1,0:T(8,128)S(1)}, bf16[1024,7168]{1,0:T(8,128)(2,1)S(1)}, bf16[8,56]{1,0:T(8,128)(2,1)S(1)}) custom-call(bf16[448,2048]{1,0:T(8,128)(2,1)} %bitcast.3, bf16[1024,7168]{1,0:T(8,128)(2,1)} %hidden.1, s32[8,128]{1,0:T(8,128)} %bitcast.4, s32[1]{0:T(128)S(6)} %copy.7.counts), custom_call_target="tpu_custom_call" | custom-call | flops 15032385536 | bytes 29360128 | tf_op jit(solution)/shard_map/refresh/pallas_call | solution.py:363
  82.3 5.3 %write.1 = (bf16[1024,7168]{1,0:T(8,128)(2,1)}, f32[8,128]{1,0:T(8,128)}, bf16[8,56]{1,0:T(8,128)(2,1)}) custom-call(bf16[1024,7168]{1,0:T(8,128)(2,1)S(1)} %get-tuple-element.9.held, f32[8,128]{1,0:T(8,128)S(1)} %get-tuple-element.10.held_logprob, bf16[8,56]{1,0:T(8,128)(2,1)S(1)} %get-tuple-element.11.held_scale), custom_call_target="tpu_custom_call" | custom-call | bytes 29360128 | tf_op jit(solution)/shard_map/write/pallas_call | solution.py:397

commit v5 on v4

--- a/solution.py
+++ b/solution.py
@@ -30,7 +30,7 @@
     logprob, quant, scale,
     arrived, states, scales, logits, wanted, parts, stats,
     a2a_send, a2a_recv, hid_sem, tgt_sem, near_recv, near_send,
-    own_send, fwd_send, core_send, sc_send, st_send,
+    own_send, fwd_send, core_send, sc_send, st_send, early_recv,
     prev_recv, next_recv, top_recv, bot_recv, core_recv, sc_recv, st_recv,
 ):
     g = lax.axis_index("group")
@@ -103,10 +103,10 @@
             tile = jnp.where(lane == p * BLOCKS + first + i, jnp.broadcast_to(s, (1, QB)), tile)
         scales[e, g] = tile
 
-    def send_own(k, at, width):
+    def send_own(k, at, width, early=False):
         block = quant.at[rows(g), pl.ds(pl.multiple_of(at, QB), width)]
-        remote(block, block, own_send.at[0, k], prev_recv.at[k], (gn, t))
-        remote(block, block, own_send.at[1, k], next_recv.at[k], (gp, t))
+        remote(block, block, own_send.at[0, k], early_recv.at[0] if early else prev_recv.at[k], (gn, t))
+        remote(block, block, own_send.at[1, k], early_recv.at[1] if early else next_recv.at[k], (gp, t))
         remote(block, block, core_send.at[0, k], core_recv.at[0, k], (go, t))
 
     def send_scales(e):
@@ -149,11 +149,35 @@
         scales[e, g] = jnp.zeros((1, QB), jnp.float32)
     wait(arrived.at[block_of(t)], a2a_recv.at[t])
     quantize(0, 4 * odd, 3)
-    send_own(0, p0 * CW + 4 * odd * QB, 3 * QB)
+    send_own(0, p0 * CW + 4 * odd * QB, 3 * QB, early=True)
     for j in range(1, AHEAD):
         send_pair(j)
     pltpu.make_async_copy(hidden, states, hid_sem).start()
     logits[...] = jnp.zeros_like(logits)
+
+    def forward(k, at):
+        wait(quant.at[rows(gp), at], early_recv.at[0] if k is None else prev_recv.at[k])
+        k0 = 0 if k is None else k
+        top = quant.at[rows(gp, 0, HALF), at]
+        remote(top, top, fwd_send.at[0, k0], top_recv.at[k0], (gn, t))
+        wait(quant.at[rows(gn), at], early_recv.at[1] if k is None else next_recv.at[k])
+        bot = quant.at[rows(gn, HALF, HALF), at]
+        remote(bot, bot, fwd_send.at[1, k0], bot_recv.at[k0], (gp, t))
+
+    def step_near(k):
+        p = pair(k)
+
+        @pl.when(k == 0)
+        def _():
+            forward(k, pl.ds(pl.multiple_of(p * CW + (3 - 3 * odd) * QB, QB), 4 * QB))
+
+        @pl.when(k > 0)
+        def _():
+            forward(k, cols(p))
+
+        for n, b in ((1, gp), (2, gn)):
+            block = quant.at[rows(b), cols(p)]
+            remote(block, block, core_send.at[n, k], core_recv.at[n, k], (go, t))
 
     for part in (True, False):
         at, size = near_part(other, 1 - odd, part)
@@ -162,6 +186,8 @@
         quantize(0, first, 2)
         send_own(0, p0 * CW + first * QB, 2 * QB)
 
+    forward(None, pl.ds(pl.multiple_of(p0 * CW + 4 * odd * QB, QB), 3 * QB))
+
     def step_own(k):
         p = pair(k)
         wait(arrived.at[block_of(2 * p)], a2a_recv.at[2 * p])
@@ -173,19 +199,6 @@
             send_scales(batch(k))
 
         send_own(k, p * CW, CW)
-
-    def step_near(k):
-        p = pair(k)
-        block = quant.at[rows(gp), cols(p)]
-        wait(block, prev_recv.at[k])
-        top = quant.at[rows(gp, 0, HALF), cols(p)]
-        remote(top, top, fwd_send.at[0, k], top_recv.at[k], (gn, t))
-        remote(block, block, core_send.at[1, k], core_recv.at[1, k], (go, t))
-        block = quant.at[rows(gn), cols(p)]
-        wait(block, next_recv.at[k])
-        bot = quant.at[rows(gn, HALF, HALF), cols(p)]
-        remote(bot, bot, fwd_send.at[1, k], bot_recv.at[k], (gp, t))
-        remote(block, block, core_send.at[2, k], core_recv.at[2, k], (go, t))
 
     def step_far(k):
         p = pair(k)
@@ -378,7 +391,7 @@
             pltpu.VMEM((NZ, 2, 8, QB), jnp.float32),
             pltpu.VMEM((NT, 2, 8, QB), jnp.float32),
             dma((NT,)), dma((NT,)), dma(()), dma(()), dma(()), dma(()),
-            dma((2, NP)), dma((2, NP)), dma((4, NP)), dma((NP // 2,)), dma(()),
+            dma((2, NP)), dma((2, NP)), dma((4, NP)), dma((NP // 2,)), dma(()), dma((2,)),
             dma((NP,)), dma((NP,)), dma((NP,)), dma((NP,)), dma((4, NP)), dma((NP // 2,)), dma(()),
         ],
         compiler_params=pltpu.CompilerParams(

time: 88.8 us -> 87.9 us (0.990)
  Pallas kernels: 86.3 us -> 85.4 us
    pallas_call x1, Pallas kernels: 81 us -> 80.1 us  [local(): pl.pallas_call(kernel, out_shape=(pltpu.VMEM((8, QB), jnp.float32), pltpu...]
where the time goes in v5:
time: 87.9 us; the launch traced here: 86.7 us
  Pallas kernels  85.4 us (97%)
  between operations  1.29 us (1%)
    pallas_call x1, Pallas kernels, local(): pl.pallas_call(kernel, out_shape=(pltpu.VMEM((8, QB), jnp.float32), pltpu...  80.1 us
    pallas_call x1, Pallas kernels, local(): pl.pallas_call(write, out_shape=(pltpu.HBM((ROWS, D), jnp.bfloat16), pltp...  5.34 us

profile of v5, /device:TPU:0, one launch (start us, length us, event | category | flops | bytes accessed | tf_op | source)
XLA Modules:
  0.0 86.7 jit_solution(17639401497745689491)
XLA Ops:
  1.3 80.1 %refresh.1 = (f32[8,128]{1,0:T(8,128)S(1)}, bf16[1024,7168]{1,0:T(8,128)(2,1)S(1)}, bf16[8,56]{1,0:T(8,128)(2,1)S(1)}) custom-call(bf16[448,2048]{1,0:T(8,128)(2,1)} %bitcast.3, bf16[1024,7168]{1,0:T(8,128)(2,1)} %hidden.1, s32[8,128]{1,0:T(8,128)} %bitcast.4, s32[1]{0:T(128)S(6)} %copy.7.counts), custom_call_target="tpu_custom_call" | custom-call | flops 15032385536 | bytes 29360128 | tf_op jit(solution)/shard_map/refresh/pallas_call | solution.py:376
  81.4 5.3 %write.1 = (bf16[1024,7168]{1,0:T(8,128)(2,1)}, f32[8,128]{1,0:T(8,128)}, bf16[8,56]{1,0:T(8,128)(2,1)}) custom-call(bf16[1024,7168]{1,0:T(8,128)(2,1)S(1)} %get-tuple-element.9.held, f32[8,128]{1,0:T(8,128)S(1)} %get-tuple-element.10.held_logprob, bf16[8,56]{1,0:T(8,128)(2,1)S(1)} %get-tuple-element.11.held_scale), custom_call_target="tpu_custom_call" | custom-call | bytes 29360128 | tf_op jit(solution)/shard_map/write/pallas_call | solution.py:410

commit v6 on v5

--- a/solution.py
+++ b/solution.py
@@ -19,9 +19,9 @@
 CW = 2 * SRC
 BLOCKS = CW // QB
 HALF = QB // 2
-LEAD = 2
+LEAD = 3
 AHEAD = 4
-LAG = 2
+LAG = 3
 VMEM_LIMIT = 32 << 20
 
 

time: 87.9 us -> 87.3 us (level); the launches traced: 86.7 us -> 87 us
  no operation moved by 1% of the time
where the time goes in v6:
time: 87.3 us; the launch traced here: 87 us
  Pallas kernels  85.8 us (98%)
  between operations  1.29 us (1%)
    pallas_call x1, Pallas kernels, local(): pl.pallas_call(kernel, out_shape=(pltpu.VMEM((8, QB), jnp.float32), pltpu...  80.4 us
    pallas_call x1, Pallas kernels, local(): pl.pallas_call(write, out_shape=(pltpu.HBM((ROWS, D), jnp.bfloat16), pltp...  5.34 us

profile of v6, /device:TPU:0, one launch (start us, length us, event | category | flops | bytes accessed | tf_op | source)
XLA Modules:
  0.0 87.0 jit_solution(11472552370388962598)
XLA Ops:
  1.3 80.4 %refresh.1 = (f32[8,128]{1,0:T(8,128)S(1)}, bf16[1024,7168]{1,0:T(8,128)(2,1)S(1)}, bf16[8,56]{1,0:T(8,128)(2,1)S(1)}) custom-call(bf16[448,2048]{1,0:T(8,128)(2,1)} %bitcast.3, bf16[1024,7168]{1,0:T(8,128)(2,1)} %hidden.1, s32[8,128]{1,0:T(8,128)} %bitcast.4, s32[1]{0:T(128)S(6)} %copy.7.counts), custom_call_target="tpu_custom_call" | custom-call | flops 15032385536 | bytes 29360128 | tf_op jit(solution)/shard_map/refresh/pallas_call | solution.py:376
  81.7 5.3 %write.1 = (bf16[1024,7168]{1,0:T(8,128)(2,1)}, f32[8,128]{1,0:T(8,128)}, bf16[8,56]{1,0:T(8,128)(2,1)}) custom-call(bf16[1024,7168]{1,0:T(8,128)(2,1)S(1)} %get-tuple-element.9.held, f32[8,128]{1,0:T(8,128)S(1)} %get-tuple-element.10.held_logprob, bf16[8,56]{1,0:T(8,128)(2,1)S(1)} %get-tuple-element.11.held_scale), custom_call_target="tpu_custom_call" | custom-call | bytes 29360128 | tf_op jit(solution)/shard_map/write/pallas_call | solution.py:410

commit v7 on v6

--- a/solution.py
+++ b/solution.py
@@ -164,20 +164,14 @@
         bot = quant.at[rows(gn, HALF, HALF), at]
         remote(bot, bot, fwd_send.at[1, k0], bot_recv.at[k0], (gp, t))
 
+    def copy_near(k):
+        for n, b in ((1, gp), (2, gn)):
+            block = quant.at[rows(b), cols(pair(k))]
+            remote(block, block, core_send.at[n, k], core_recv.at[n, k], (go, t))
+
     def step_near(k):
-        p = pair(k)
-
-        @pl.when(k == 0)
-        def _():
-            forward(k, pl.ds(pl.multiple_of(p * CW + (3 - 3 * odd) * QB, QB), 4 * QB))
-
-        @pl.when(k > 0)
-        def _():
-            forward(k, cols(p))
-
-        for n, b in ((1, gp), (2, gn)):
-            block = quant.at[rows(b), cols(p)]
-            remote(block, block, core_send.at[n, k], core_recv.at[n, k], (go, t))
+        forward(k, cols(pair(k)))
+        copy_near(k)
 
     for part in (True, False):
         at, size = near_part(other, 1 - odd, part)
@@ -246,6 +240,9 @@
             send_scales(0)
         send_own(1, p1 * CW + first * QB, count * QB)
     send_pair(AHEAD)
+
+    forward(0, pl.ds(pl.multiple_of(p0 * CW + (3 - 3 * odd) * QB, QB), 4 * QB))
+    copy_near(0)
     for k in range(2, LEAD):
         send_pair(AHEAD - 1 + k)
         step_own(jnp.int32(k))
@@ -264,7 +261,9 @@
         def _():
             dot_own(k)
 
-        step_near(k)
+        @pl.when(k > 0)
+        def _():
+            step_near(k)
 
         @pl.when(k >= LAG)
         def _():

time: 87.3 us -> 87.3 us (level)
  no operation moved by 1% of the time
where the time goes in v7:
time: 87.3 us; the launch traced here: 87.1 us
  Pallas kernels  85.8 us (98%)
  between operations  1.29 us (1%)
    pallas_call x1, Pallas kernels, local(): pl.pallas_call(kernel, out_shape=(pltpu.VMEM((8, QB), jnp.float32), pltpu...  80.4 us
    pallas_call x1, Pallas kernels, local(): pl.pallas_call(write, out_shape=(pltpu.HBM((ROWS, D), jnp.bfloat16), pltp...  5.34 us

profile of v7, /device:TPU:0, one launch (start us, length us, event | category | flops | bytes accessed | tf_op | source)
XLA Modules:
  0.0 87.1 jit_solution(17335880787859120183)
XLA Ops:
  1.3 80.4 %refresh.1 = (f32[8,128]{1,0:T(8,128)S(1)}, bf16[1024,7168]{1,0:T(8,128)(2,1)S(1)}, bf16[8,56]{1,0:T(8,128)(2,1)S(1)}) custom-call(bf16[448,2048]{1,0:T(8,128)(2,1)} %bitcast.3, bf16[1024,7168]{1,0:T(8,128)(2,1)} %hidden.1, s32[8,128]{1,0:T(8,128)} %bitcast.4, s32[1]{0:T(128)S(6)} %copy.7.counts), custom_call_target="tpu_custom_call" | custom-call | flops 15032385536 | bytes 29360128 | tf_op jit(solution)/shard_map/refresh/pallas_call | solution.py:375
  81.7 5.3 %write.1 = (bf16[1024,7168]{1,0:T(8,128)(2,1)}, f32[8,128]{1,0:T(8,128)}, bf16[8,56]{1,0:T(8,128)(2,1)}) custom-call(bf16[1024,7168]{1,0:T(8,128)(2,1)S(1)} %get-tuple-element.9.held, f32[8,128]{1,0:T(8,128)S(1)} %get-tuple-element.10.held_logprob, bf16[8,56]{1,0:T(8,128)(2,1)S(1)} %get-tuple-element.11.held_scale), custom_call_target="tpu_custom_call" | custom-call | bytes 29360128 | tf_op jit(solution)/shard_map/write/pallas_call | solution.py:409
